TPU v7x, 32 devices: a whole 2x2x4 slice. The times are simulated.
32 devices in a mesh: dp: 16 (over z, y, x), feat: 2 (over core).
Axes of the slice: x: 2, y: 2, z: 4, core: 2. Of those that a mesh axis runs over, the one named last changes fastest.
Arguments:
- inputs: float32 [20480, 640], P('dp', 'feat'), may hold values from -6 to 6
- encoder: bfloat16 [20480, 640], P('dp', 'feat'), may hold values from -6 to 6
- output_grad: float32 [20480, 640], P('dp', 'feat'), may hold values from -6 to 6
- target_lengths: int32 [32, 24], P(('dp', 'feat')), may hold values from 0 to 256, as said below
- source_lengths: int32 [32, 24], P(('dp', 'feat')), may hold values from 0 to 256, as said below
- gains: float32 [3, 640], P(None, 'feat'), may hold values from 0.5 to 1.5
- shifts: float32 [3, 640], P(None, 'feat'), may hold values from -2 to 2
- self_inproj: bfloat16 [640, 1920], replicated, may hold values from -0.25 to 0.25
- self_outproj: bfloat16 [640, 640], replicated, may hold values from -1 to 1
- cross_query: bfloat16 [640, 640], replicated, may hold values from -0.25 to 0.25
- cross_keyvalue: bfloat16 [640, 1280], replicated, may hold values from -0.25 to 0.25
- cross_outproj: bfloat16 [640, 640], replicated, may hold values from -1 to 1
- ffn_expand: bfloat16 [640, 3072], replicated, may hold values from -0.25 to 0.25
- ffn_reduce: bfloat16 [3072, 640], replicated, may hold values from -0.109375 to 0.109375
Outputs:
- layer_out: float32 [20480, 640], P('dp', 'feat')
- input_grad: float32 [20480, 640], P('dp', 'feat')
- encoder_grad: float32 [20480, 640], P('dp', 'feat')
- gain_grad: float32 [3, 640], P(None, 'feat')
- shift_grad: float32 [3, 640], P(None, 'feat')
- self_inproj_grad: float32 [640, 1920], P('dp', 'feat')
- self_outproj_grad: float32 [640, 640], P('dp', 'feat')
- cross_query_grad: float32 [640, 640], P('dp', 'feat')
- cross_keyvalue_grad: float32 [640, 1280], P('dp', 'feat')
- cross_outproj_grad: float32 [640, 640], P('dp', 'feat')
- ffn_expand_grad: float32 [640, 3072], P('dp', 'feat')
- ffn_reduce_grad: float32 [3072, 640], P('dp', 'feat')
Inputs may be any that keep to these rules, and one draw needn't show every extreme that they name: `target_lengths`: in each bucket the nonzero lengths fill the first slots and zeros the rest; a bucket's lengths sum to 640 or less; in every draw one bucket, chosen from the seed, has a first sentence of 256. `source_lengths`: nonzero exactly where target_lengths is, and at most the target length.
All inputs are finite; a program needn't handle non-finite values.
Results may differ from a plain program's by a relative error of at most 0.017.
Values may be sent and summed in bfloat16 or wider, within the bound.
A program may use at most 192 MiB of HBM per device.

v0:
```python
import math

import jax
import jax.numpy as jnp
from jax import lax
from jax.sharding import PartitionSpec as P

HEADS = 8


EPSILON = 1e-05
MASKED_SCORE = -1e30


def as_sent(array):

    def short(part):
        return part.astype(jnp.bfloat16) if part.dtype == jnp.float32 else part

    return jax.tree.map(short, array)


def inner(left, right):
    return lax.dot_general(
        left, right, (((0,), (0,)), ((), ())), preferred_element_type=jnp.float32
    )


def backward_product(grad, weight):
    return lax.dot_general(
        grad, weight, (((1,), (1,)), ((), ())), preferred_element_type=jnp.float32
    )


def smooth_gate(values):
    return jax.nn.gelu(values, approximate=True)


def row_sums(first, second):
    return lax.psum((first, second), "feat")


def to_tokens(parts):
    return jax.tree.map(
        lambda part, own: part.astype(own.dtype),
        lax.all_to_all(as_sent(parts), "feat", split_axis=0, concat_axis=1, tiled=True),
        parts,
    )


def to_features(parts):
    return jax.tree.map(
        lambda part, own: part.astype(own.dtype),
        lax.all_to_all(as_sent(parts), "feat", split_axis=1, concat_axis=0, tiled=True),
        parts,
    )


def norm_forward(values, gain, shift):
    width = values.shape[1] * lax.axis_size("feat")
    total, squares = row_sums(jnp.sum(values, axis=1), jnp.sum(values * values, axis=1))
    center = total / width
    reciprocal = lax.rsqrt(squares / width - center * center + EPSILON)
    normed = (values - center[:, None]) * reciprocal[:, None]
    return (normed, reciprocal, (normed * gain + shift).astype(jnp.bfloat16))


def norm_backward(grad_normed, normed, reciprocal, gain):
    width = normed.shape[1] * lax.axis_size("feat")
    grad_value = grad_normed.astype(jnp.float32)
    scaled = grad_value * gain
    first, second = row_sums(jnp.sum(scaled, axis=1), jnp.sum(scaled * normed, axis=1))
    grad_input = reciprocal[:, None] * (
        scaled - first[:, None] / width - normed * (second[:, None] / width)
    )
    return (grad_input, jnp.sum(grad_value * normed, axis=0), jnp.sum(grad_value, axis=0))


def sentence_rows(lengths, count):
    ends = jnp.cumsum(lengths[0], dtype=jnp.int32)
    positions = jnp.arange(count, dtype=jnp.int32)
    sentence = jnp.sum(
        (ends[None, :] <= positions[:, None]).astype(jnp.int32), axis=1, dtype=jnp.int32
    )
    return (sentence, positions < ends[-1])


def split_heads(values):
    return values.reshape(values.shape[0], HEADS, values.shape[1] // HEADS)


def head_scores(queries, keys, allowed):
    head_size = queries.shape[1] // HEADS
    scores = jnp.einsum(
        "qhd,khd->hqk", split_heads(queries), split_heads(keys), preferred_element_type=jnp.float32
    ) * (1.0 / math.sqrt(head_size))
    return jnp.where(allowed[None, :, :], scores, MASKED_SCORE)


def attend_forward(queries, keys, values, allowed):
    scores = head_scores(queries, keys, allowed)
    largest = jnp.max(scores, axis=-1, keepdims=True)
    expo = jnp.exp(scores - largest)
    total = jnp.sum(expo, axis=-1, keepdims=True)
    weights = expo / total
    mixed = jnp.einsum(
        "hqk,khd->qhd",
        weights.astype(jnp.bfloat16),
        split_heads(values),
        preferred_element_type=jnp.float32,
    )
    log_total = largest[..., 0] + jnp.log(total[..., 0])
    return (mixed.reshape(queries.shape).astype(jnp.bfloat16), log_total)


def attend_backward(queries, keys, values, allowed, log_total, grad_mixed):
    head_size = queries.shape[1] // HEADS
    scale = 1.0 / math.sqrt(head_size)
    weights = jnp.exp(head_scores(queries, keys, allowed) - log_total[..., None])
    grad_heads = split_heads(grad_mixed)
    grad_weights = jnp.einsum(
        "qhd,khd->hqk", grad_heads, split_heads(values), preferred_element_type=jnp.float32
    )
    grad_values = jnp.einsum(
        "hqk,qhd->khd", weights.astype(jnp.bfloat16), grad_heads, preferred_element_type=jnp.float32
    )
    centre = jnp.sum(weights * grad_weights, axis=-1, keepdims=True)
    grad_scores = (weights * (grad_weights - centre)).astype(jnp.bfloat16)
    grad_queries = (
        jnp.einsum(
            "hqk,khd->qhd", grad_scores, split_heads(keys), preferred_element_type=jnp.float32
        )
        * scale
    )
    grad_keys = (
        jnp.einsum(
            "hqk,qhd->khd", grad_scores, split_heads(queries), preferred_element_type=jnp.float32
        )
        * scale
    )
    return (
        grad_queries.reshape(queries.shape),
        grad_keys.reshape(keys.shape),
        grad_values.reshape(values.shape),
    )


def masked_rows(grad, valid):
    return jnp.where(valid[:, None], grad, jnp.zeros_like(grad))


def per_device(
    inputs,
    encoder,
    output_grad,
    target_lengths,
    source_lengths,
    gains,
    shifts,
    self_inproj,
    self_outproj,
    cross_query,
    cross_keyvalue,
    cross_outproj,
    ffn_expand,
    ffn_reduce,
):
    count = inputs.shape[0] // lax.axis_size("feat")
    width = self_outproj.shape[0]
    target_seg, target_valid = sentence_rows(target_lengths, count)
    source_seg, source_valid = sentence_rows(source_lengths, count)
    positions = jnp.arange(count, dtype=jnp.int32)
    keep = target_valid.astype(jnp.float32)[:, None]
    self_mask = (target_seg[:, None] == target_seg[None, :]) & (
        positions[None, :] <= positions[:, None]
    )
    self_mask = self_mask & target_valid[:, None] & target_valid[None, :]
    cross_mask = (
        (target_seg[:, None] == source_seg[None, :]) & target_valid[:, None] & source_valid[None, :]
    )
    normed_one, recip_one, normed_cols = norm_forward(inputs, gains[0], shifts[0])
    (normed1,) = to_tokens((normed_cols,))
    projected = jnp.dot(normed1, self_inproj, preferred_element_type=jnp.float32).astype(
        jnp.bfloat16
    )
    queries = projected[:, :width]
    keys = projected[:, width : 2 * width]
    values = projected[:, 2 * width :]
    attended1, log_one = attend_forward(queries, keys, values, self_mask)
    branch = (jnp.dot(attended1, self_outproj, preferred_element_type=jnp.float32) * keep).astype(
        jnp.bfloat16
    )
    (branch_cols,) = to_features((branch,))
    mid_one = inputs + branch_cols.astype(jnp.float32)
    normed_two, recip_two, normed_cols = norm_forward(mid_one, gains[1], shifts[1])
    normed2, source_rows = to_tokens((normed_cols, encoder))
    cross_queries = jnp.dot(normed2, cross_query, preferred_element_type=jnp.float32).astype(
        jnp.bfloat16
    )
    memory = jnp.dot(source_rows, cross_keyvalue, preferred_element_type=jnp.float32).astype(
        jnp.bfloat16
    )
    attended2, log_two = attend_forward(
        cross_queries, memory[:, :width], memory[:, width:], cross_mask
    )
    branch = (jnp.dot(attended2, cross_outproj, preferred_element_type=jnp.float32) * keep).astype(
        jnp.bfloat16
    )
    (branch_cols,) = to_features((branch,))
    mid_two = mid_one + branch_cols.astype(jnp.float32)
    normed_three, recip_three, normed_cols = norm_forward(mid_two, gains[2], shifts[2])
    (normed3,) = to_tokens((normed_cols,))
    expanded = jnp.dot(normed3, ffn_expand, preferred_element_type=jnp.float32).astype(jnp.bfloat16)
    gated, gate_pull = jax.vjp(smooth_gate, expanded.astype(jnp.float32))
    activated = gated.astype(jnp.bfloat16)
    branch = (jnp.dot(activated, ffn_reduce, preferred_element_type=jnp.float32) * keep).astype(
        jnp.bfloat16
    )
    (branch_cols,) = to_features((branch,))
    layer_out = mid_two + branch_cols.astype(jnp.float32)
    (grad_branch,) = to_tokens((output_grad.astype(jnp.bfloat16),))
    grad_branch = masked_rows(grad_branch, target_valid)
    reduce_grad = inner(activated, grad_branch)
    grad_act = backward_product(grad_branch, ffn_reduce)
    (grad_pre,) = gate_pull(grad_act)
    grad_expanded = grad_pre.astype(jnp.bfloat16)
    expand_grad = inner(normed3, grad_expanded)
    grad_normed = backward_product(grad_expanded, ffn_expand).astype(jnp.bfloat16)
    (grad_cols,) = to_features((grad_normed,))
    part_three, gain_three, shift_three = norm_backward(
        grad_cols, normed_three, recip_three, gains[2]
    )
    grad_mid_two = output_grad + part_three
    (grad_branch,) = to_tokens((grad_mid_two.astype(jnp.bfloat16),))
    grad_branch = masked_rows(grad_branch, target_valid)
    cross_out_grad = inner(attended2, grad_branch)
    grad_attended = backward_product(grad_branch, cross_outproj).astype(jnp.bfloat16)
    grad_cq, grad_ck, grad_cv = attend_backward(
        cross_queries, memory[:, :width], memory[:, width:], cross_mask, log_two, grad_attended
    )
    grad_cq = grad_cq.astype(jnp.bfloat16)
    grad_memory = jnp.concatenate([grad_ck, grad_cv], axis=1).astype(jnp.bfloat16)
    cross_query_grad = inner(normed2, grad_cq)
    cross_kv_grad = inner(source_rows, grad_memory)
    grad_normed = backward_product(grad_cq, cross_query).astype(jnp.bfloat16)
    grad_source = backward_product(grad_memory, cross_keyvalue).astype(jnp.bfloat16)
    grad_cols, grad_source_cols = to_features((grad_normed, grad_source))
    part_two, gain_two, shift_two = norm_backward(grad_cols, normed_two, recip_two, gains[1])
    grad_mid_one = grad_mid_two + part_two
    (grad_branch,) = to_tokens((grad_mid_one.astype(jnp.bfloat16),))
    grad_branch = masked_rows(grad_branch, target_valid)
    self_out_grad = inner(attended1, grad_branch)
    grad_attended = backward_product(grad_branch, self_outproj).astype(jnp.bfloat16)
    grad_q, grad_k, grad_v = attend_backward(
        queries, keys, values, self_mask, log_one, grad_attended
    )
    grad_projected = jnp.concatenate([grad_q, grad_k, grad_v], axis=1).astype(jnp.bfloat16)
    self_in_grad = inner(normed1, grad_projected)
    grad_normed = backward_product(grad_projected, self_inproj).astype(jnp.bfloat16)
    (grad_cols,) = to_features((grad_normed,))
    part_one, gain_one, shift_one = norm_backward(grad_cols, normed_one, recip_one, gains[0])
    input_grad = grad_mid_one + part_one
    gain_local = jnp.stack([gain_one, gain_two, gain_three], axis=0)
    shift_local = jnp.stack([shift_one, shift_two, shift_three], axis=0)
    gain_grad, shift_grad = lax.psum((gain_local, shift_local), "dp")
    weight_terms = (
        self_in_grad,
        self_out_grad,
        cross_query_grad,
        cross_kv_grad,
        cross_out_grad,
        expand_grad,
        reduce_grad,
    )
    summed_rows = (
        lax.psum_scatter(weight_terms[0], "dp", scatter_dimension=0, tiled=True),
        lax.psum_scatter(weight_terms[1], "dp", scatter_dimension=0, tiled=True),
        lax.psum_scatter(weight_terms[2], "dp", scatter_dimension=0, tiled=True),
        lax.psum_scatter(weight_terms[3], "dp", scatter_dimension=0, tiled=True),
        lax.psum_scatter(weight_terms[4], "dp", scatter_dimension=0, tiled=True),
        lax.psum_scatter(weight_terms[5], "dp", scatter_dimension=0, tiled=True),
        lax.psum_scatter(weight_terms[6], "dp", scatter_dimension=0, tiled=True),
    )
    summed = (
        lax.psum_scatter(
            summed_rows[0].astype(jnp.bfloat16), "feat", scatter_dimension=1, tiled=True
        ).astype(jnp.float32),
        lax.psum_scatter(
            summed_rows[1].astype(jnp.bfloat16), "feat", scatter_dimension=1, tiled=True
        ).astype(jnp.float32),
        lax.psum_scatter(
            summed_rows[2].astype(jnp.bfloat16), "feat", scatter_dimension=1, tiled=True
        ).astype(jnp.float32),
        lax.psum_scatter(
            summed_rows[3].astype(jnp.bfloat16), "feat", scatter_dimension=1, tiled=True
        ).astype(jnp.float32),
        lax.psum_scatter(
            summed_rows[4].astype(jnp.bfloat16), "feat", scatter_dimension=1, tiled=True
        ).astype(jnp.float32),
        lax.psum_scatter(
            summed_rows[5].astype(jnp.bfloat16), "feat", scatter_dimension=1, tiled=True
        ).astype(jnp.float32),
        lax.psum_scatter(
            summed_rows[6].astype(jnp.bfloat16), "feat", scatter_dimension=1, tiled=True
        ).astype(jnp.float32),
    )
    return (
        layer_out,
        input_grad,
        grad_source_cols.astype(jnp.float32),
        gain_grad,
        shift_grad,
        summed[0],
        summed[1],
        summed[2],
        summed[3],
        summed[4],
        summed[5],
        summed[6],
    )


def solution(mesh):
    in_specs = (
        P("dp", "feat"),
        P("dp", "feat"),
        P("dp", "feat"),
        P(("dp", "feat"), None),
        P(("dp", "feat"), None),
        P(None, "feat"),
        P(None, "feat"),
        P(),
        P(),
        P(),
        P(),
        P(),
        P(),
        P(),
    )
    out_specs = (
        P("dp", "feat"),
        P("dp", "feat"),
        P("dp", "feat"),
        P(None, "feat"),
        P(None, "feat"),
        P("dp", "feat"),
        P("dp", "feat"),
        P("dp", "feat"),
        P("dp", "feat"),
        P("dp", "feat"),
        P("dp", "feat"),
        P("dp", "feat"),
    )
    return jax.shard_map(
        per_device, mesh=mesh, in_specs=in_specs, out_specs=out_specs, check_vma=False
    )
```

profile of v0, /device:TPU:0, one launch (start us, length us, event | category | flops | bytes accessed | tf_op | source)
XLA Modules:
  0.0 1086.2 jit_solution(17198916927926176433)
XLA Ops:
  123.6 8.5 fusion.54
  132.1 12.6 %fusion.7 = (bf16[640,3072]{1,0:T(8,128)(2,1)}, bf16[640,3072]{1,0:T(8,128)(2,1)S(1)}) fusion(f32[640,3072]{1,0:T(8,128)} %fusion.54, bf16[640,640]{0,1:T(8,128)(2,1)S(1)} %bitcast.254, bf16[640,3072]{1,0:T(8,128)(2,1)} %param.26), kind=kOutput, calls=%fused_computation.24 | convolution fusion | flops 2559836160 | bytes 20480000 | tf_op jit(solution)/shard_map/dot_general | solution.py:213
  153.4 7.5 convolution_convert_fusion.8
  188.5 12.1 %multiply_reduce_fusion.1 = (f32[8,640]{1,0:T(8,128)S(1)}, f32[8,640,640]{1,2,0:T(8,128)}) fusion(f32[8,640,640]{1,2,0:T(8,128)} %copy-done.2, f32[8,640]{1,0:T(8,128)S(1)} %log_add_fusion.1, bf16[640,8,80]{0,2,1:T(8,128)(2,1)S(1)} %bitcast.240, bf16[640,8,80]{0,2,1:T(8,128)(2,1)S(1)} %bitcast.237), kind=kOutput, calls=%fused_computation.9 | convolution fusion | flops 534113280 | bytes 27893760 | tf_op jit(solution)/shard_map/qhd,khd->hqk/dot_general | solution.py:121
  201.7 6.6 multiply_convert_fusion.1
  243.8 5.4 multiply_convert_fusion.2
  249.2 7.3 fusion.28
  269.9 12.0 %multiply_reduce_fusion = (f32[8,640]{1,0:T(8,128)S(1)}, f32[8,640,640]{1,2,0:T(8,128)}) fusion(f32[8,640,640]{1,2,0:T(8,128)} %copy-done.1, f32[8,640]{1,0:T(8,128)S(1)} %log_add_fusion, bf16[640,8,80]{0,2,1:T(8,128)(2,1)S(1)} %bitcast.242, bf16[640,8,80]{0,2,1:T(8,128)(2,1)S(1)} %bitcast.235), kind=kOutput, calls=%fused_computation.6 | convolution fusion | flops 534113280 | bytes 27893760 | tf_op jit(solution)/shard_map/qhd,khd->hqk/dot_general | solution.py:121
  282.8 6.6 multiply_convert_fusion
  301.7 10.3 fusion.42
  312.1 8.7 fusion.58
  335.0 40.3 %reduce-scatter.64.cloned.1.call-done = f32[40,640]{1,0:T(8,128)} async-done(((f32[640,640]{1,0:T(8,128)}), f32[40,640]{1,0:T(8,128)}) %reduce-scatter.64.cloned.1.call-update) | async-done | bytes 102416
  382.7 70.9 %reduce-scatter.60.cloned.1.call-done = f32[40,640]{1,0:T(8,128)} async-done(((f32[640,640]{1,0:T(8,128)}), f32[40,640]{1,0:T(8,128)}) %reduce-scatter.60.cloned.1.call-update) | async-done | bytes 102416
  458.6 78.9 %reduce-scatter.52.cloned.1.call-done = f32[40,1280]{1,0:T(8,128)} async-done(((f32[640,1280]{1,0:T(8,128)}), f32[40,1280]{1,0:T(8,128)}) %reduce-scatter.52.cloned.1.call-update) | async-done | bytes 204816
  542.1 136.9 %reduce-scatter.58.cloned.1.call-done = f32[40,1920]{1,0:T(8,128)} async-done(((f32[640,1920]{1,0:T(8,128)}), f32[40,1920]{1,0:T(8,128)}) %reduce-scatter.58.cloned.1.call-update) | async-done | bytes 307216
  683.5 156.5 %reduce-scatter.44.cloned.1.call-done = f32[192,640]{1,0:T(8,128)} async-done(((f32[3072,640]{1,0:T(8,128)}), f32[192,640]{1,0:T(8,128)}) %reduce-scatter.44.cloned.1.call-update) | async-done | bytes 491536 | tf_op jit(solution)/shard_map/reduce_scatter | solution.py:282
  844.8 75.8 %all-reduce.4 = (f32[3,320]{1,0:T(4,128)}, f32[3,320]{1,0:T(4,128)}) all-reduce(f32[3,320]{1,0:T(4,128)S(1)} %pad_maximum_fusion.6, f32[3,320]{1,0:T(4,128)S(1)} %pad_maximum_fusion.7), channel_id=1, replica_groups=mesh['dp'=16,'feat'=2] {'dp'}, use_global_device_ids=true, to_apply=%region_37.38 | all-reduce | flops 1920 | bytes 15360 | tf_op jit(solution)/shard_map/psum | solution.py:265
  923.9 76.5 %reduce-scatter.40.cloned.1.call-done = f32[40,3072]{1,0:T(8,128)} async-done(((f32[640,3072]{1,0:T(8,128)}), f32[40,3072]{1,0:T(8,128)}) %reduce-scatter.40.cloned.1.call-update) | async-done | bytes 491536 | tf_op jit(solution)/shard_map/reduce_scatter | solution.py:281
  1011.5 9.5 reduce-scatter.54.cloned.1.call-done
  1022.6 9.8 reduce-scatter.48.cloned.1.call-done
  1034.1 9.6 reduce-scatter.38.cloned.1.call-done
  1045.4 9.6 reduce-scatter.46.cloned.1.call-done
  1056.7 9.4 reduce-scatter.56.cloned.1.call-done
  1067.8 9.8 reduce-scatter.42.cloned.1.call-done
  (317 shorter events, 279.9 us)
Async XLA Ops:
  16.2 7.1 all-to-all-start
  55.8 13.8 %all-to-all-start.2 = ((bf16[2,640,320]{1,2,0:T(8,128)(2,1)}), bf16[2,640,320]{1,2,0:T(8,128)(2,1)}, u32[]{:S(2)}, u32[]{:S(2)}) async-start(bf16[2,640,320]{1,2,0:T(8,128)(2,1)} %bitcast.198), calls=%async_computation.2 | async-start | bytes 1638400 | tf_op jit(solution)/shard_map/all_to_all | solution.py:46
  69.6 12.4 %all-to-all-start.3 = ((bf16[2,640,320]{1,2,0:T(8,128)(2,1)}), bf16[2,640,320]{1,2,0:T(8,128)(2,1)S(1)}, u32[]{:S(2)}, u32[]{:S(2)}) async-start(bf16[2,640,320]{1,2,0:T(8,128)(2,1)} %bitcast.224), calls=%async_computation.3 | async-start | bytes 1638400 | tf_op jit(solution)/shard_map/all_to_all | solution.py:46
  98.2 6.0 all-to-all-start.4
  104.3 13.6 %all-to-all-start.7 = ((bf16[2,640,320]{1,2,0:T(8,128)(2,1)}), bf16[2,640,320]{1,2,0:T(8,128)(2,1)}, u32[]{:S(2)}, u32[]{:S(2)}) async-start(bf16[2,640,320]{1,2,0:T(8,128)(2,1)} %bitcast.195), calls=%async_computation.7 | async-start | bytes 1638400 | tf_op jit(solution)/shard_map/all_to_all | solution.py:46
  117.9 14.2 %all-to-all-start.5 = ((bf16[2,640,320]{1,2,0:T(8,128)(2,1)}), bf16[2,640,320]{1,2,0:T(8,128)(2,1)S(1)}, u32[]{:S(2)}, u32[]{:S(2)}) async-start(bf16[2,640,320]{1,2,0:T(8,128)(2,1)} %bitcast.196), calls=%async_computation.5 | async-start | bytes 1638400 | tf_op jit(solution)/shard_map/all_to_all | solution.py:46
  149.6 11.2 %all-to-all-start.6 = ((bf16[640,2,320]{0,2,1:T(8,128)(2,1)}), bf16[640,2,320]{0,2,1:T(8,128)(2,1)S(1)}, u32[]{:S(2)}, u32[]{:S(2)}) async-start(bf16[640,2,320]{0,2,1:T(8,128)(2,1)} %bitcast.262), calls=%async_computation.6 | async-start | bytes 1638400 | tf_op jit(solution)/shard_map/all_to_all | solution.py:54
  161.8 6.1 all-to-all-start.8
  184.2 144.7 %reduce-scatter.62.cloned.1.call-start = ((), (), s32[]{:S(2)}) async-start(), calls=%async_computation.40 | async-start | bytes 1740800
  214.1 161.2 %reduce-scatter.64.cloned.1.call-start = ((), (), s32[]{:S(2)}) async-start(), calls=%async_computation.41 | async-start | bytes 1740800
  240.5 213.2 %reduce-scatter.60.cloned.1.call-start = ((), (), s32[]{:S(2)}) async-start(), calls=%async_computation.39 | async-start | bytes 1740800
  243.8 293.7 %reduce-scatter.52.cloned.1.call-start = ((), (), s32[]{:S(2)}) async-start(), calls=%async_computation.35 | async-start | bytes 3481600
  266.5 412.5 %reduce-scatter.58.cloned.1.call-start = ((), (), s32[]{:S(2)}) async-start(), calls=%async_computation.38 | async-start | bytes 5222400
  301.5 538.6 %reduce-scatter.44.cloned.1.call-start = ((), (), s32[]{:S(2)}) async-start(), calls=%async_computation.31 | async-start | bytes 8355840 | tf_op jit(solution)/shard_map/reduce_scatter | solution.py:282
  312.1 688.3 %reduce-scatter.40.cloned.1.call-start = ((), (), s32[]{:S(2)}) async-start(), calls=%async_computation.29 | async-start | bytes 8355840 | tf_op jit(solution)/shard_map/reduce_scatter | solution.py:281
  325.3 51.8 %all-to-all-start.12 = ((bf16[640,2,320]{0,2,1:T(8,128)(2,1)}), bf16[640,2,320]{0,2,1:T(8,128)(2,1)S(1)}, u32[]{:S(2)}, u32[]{:S(2)}) async-start(bf16[640,2,320]{0,2,1:T(8,128)(2,1)} %bitcast.259), calls=%async_computation.12 | async-start | bytes 1638400 | tf_op jit(solution)/shard_map/all_to_all | solution.py:54
  328.8 681.1 %reduce-scatter.50.cloned.1.call-start = ((), (), s32[]{:S(2)}) async-start(), calls=%async_computation.34 | async-start | bytes 245760
  330.6 690.4 %reduce-scatter.54.cloned.1.call-start = ((), (), s32[]{:S(2)}) async-start(), calls=%async_computation.36 | async-start | bytes 245760
  377.0 304.1 %all-to-all-start.13 = ((bf16[640,2,320]{0,2,1:T(8,128)(2,1)}), bf16[640,2,320]{0,2,1:T(8,128)(2,1)}, u32[]{:S(2)}, u32[]{:S(2)}) async-start(bf16[640,2,320]{0,2,1:T(8,128)(2,1)} %bitcast.258), calls=%async_computation.13 | async-start | bytes 1638400 | tf_op jit(solution)/shard_map/all_to_all | solution.py:54
  381.4 651.1 %reduce-scatter.48.cloned.1.call-start = ((), (), s32[]{:S(2)}) async-start(), calls=%async_computation.33 | async-start | bytes 245760
  455.4 588.3 %reduce-scatter.38.cloned.1.call-start = ((), (), s32[]{:S(2)}) async-start(), calls=%async_computation.28 | async-start | bytes 491520 | tf_op jit(solution)/shard_map/reduce_scatter | solution.py:294
  539.3 515.6 %reduce-scatter.46.cloned.1.call-start = ((), (), s32[]{:S(2)}) async-start(), calls=%async_computation.32 | async-start | bytes 737280
  681.0 385.0 %reduce-scatter.56.cloned.1.call-start = ((), (), s32[]{:S(2)}) async-start(), calls=%async_computation.37 | async-start | bytes 491520
  842.0 235.6 %reduce-scatter.42.cloned.1.call-start = ((), (), s32[]{:S(2)}) async-start(), calls=%async_computation.30 | async-start | bytes 368640 | tf_op jit(solution)/shard_map/reduce_scatter | solution.py:300
  (61 other events, 548.8 us)
Sparse Core Ops, SparseCore 0:
  214.2 81.9 reduce-scatter.61
  299.2 76.0 reduce-scatter.63
  377.6 76.0 reduce-scatter.59
  455.9 81.4 reduce-scatter.51
  543.3 135.6 reduce-scatter.57
  685.1 154.9 reduce-scatter.43
  845.4 154.9 reduce-scatter.39
  1003.2 6.6 reduce-scatter.49
  1012.2 8.7 reduce-scatter.53
  1023.7 8.6 reduce-scatter.47
  1034.8 8.8 reduce-scatter.37
  1045.8 9.0 reduce-scatter.45
  1057.1 8.8 reduce-scatter.55
  1068.8 8.7 reduce-scatter.41
where the time goes:
time: 1100 us; the launch traced here: 1090 us
  waiting for transfers between devices  624 us (57%)
  matrix products  154 us (14%)
  blocking collectives  106 us (10%)
  other arithmetic  70.9 us (6%)
  local copies, waits for them, and re-layouts  69.7 us (6%)
  starting transfers between devices  46.8 us (4%)
  between operations  15.4 us (1%)
    unnamed x24, waiting for transfers between devices  369 us
    reduce_scatter x1, waiting for transfers between devices, per_device(): lax.psum_scatter(weight_terms[6], 'dp', scatter_dimension=0, tiled=True)  156 us
    reduce_scatter x1, waiting for transfers between devices, per_device(): lax.psum_scatter(weight_terms[5], 'dp', scatter_dimension=0, tiled=True)  76.5 us
    psum x1, blocking collectives, per_device(): gain_grad, shift_grad = lax.psum((gain_local, shift_local), 'dp')  75.8 us
    unnamed x131, local copies, waits for them, and re-layouts  40.7 us
    dot_general x7, matrix products, inner(): lax.dot_general(left, right, (((0,), (0,)), ((), ())), preferred_element_...  35.2 us
    dot_general x7, matrix products, backward_product(): lax.dot_general(grad, weight, (((1,), (1,)), ((), ())), preferred_element...  31.1 us
    dot_general x2, matrix products, attend_backward(): jnp.einsum('qhd,khd->hqk', grad_heads, split_heads(values), preferred_ele...  24.1 us
  transfers between devices with their start and end apart: 26, of which 14 were waited for; matrix products, arithmetic and copies ran while one was open for 17% of the time, Pallas kernels for 0%

commit v1 on v0

--- a/solution.py
+++ b/solution.py
@@ -37,27 +37,27 @@
 
 
 def row_sums(first, second):
-    return lax.psum((first, second), "feat")
+    return (first, second)
 
 
 def to_tokens(parts):
-    return jax.tree.map(
-        lambda part, own: part.astype(own.dtype),
-        lax.all_to_all(as_sent(parts), "feat", split_axis=0, concat_axis=1, tiled=True),
-        parts,
-    )
+    return parts
 
 
 def to_features(parts):
-    return jax.tree.map(
-        lambda part, own: part.astype(own.dtype),
-        lax.all_to_all(as_sent(parts), "feat", split_axis=1, concat_axis=0, tiled=True),
-        parts,
-    )
+    return parts
+
+
+def gather_rows(part):
+    return lax.all_to_all(part, "feat", split_axis=0, concat_axis=1, tiled=True)
+
+
+def spread_rows(part):
+    return lax.all_to_all(part, "feat", split_axis=1, concat_axis=0, tiled=True)
 
 
 def norm_forward(values, gain, shift):
-    width = values.shape[1] * lax.axis_size("feat")
+    width = values.shape[1]
     total, squares = row_sums(jnp.sum(values, axis=1), jnp.sum(values * values, axis=1))
     center = total / width
     reciprocal = lax.rsqrt(squares / width - center * center + EPSILON)
@@ -66,7 +66,7 @@
 
 
 def norm_backward(grad_normed, normed, reciprocal, gain):
-    width = normed.shape[1] * lax.axis_size("feat")
+    width = normed.shape[1]
     grad_value = grad_normed.astype(jnp.float32)
     scaled = grad_value * gain
     first, second = row_sums(jnp.sum(scaled, axis=1), jnp.sum(scaled * normed, axis=1))
@@ -77,7 +77,10 @@
 
 
 def sentence_rows(lengths, count):
-    ends = jnp.cumsum(lengths[0], dtype=jnp.int32)
+    slots = jnp.arange(lengths.shape[1], dtype=jnp.int32)
+    ends = jnp.sum(
+        jnp.where(slots[:, None] <= slots[None, :], lengths[0][:, None], 0), axis=0, dtype=jnp.int32
+    )
     positions = jnp.arange(count, dtype=jnp.int32)
     sentence = jnp.sum(
         (ends[None, :] <= positions[:, None]).astype(jnp.int32), axis=1, dtype=jnp.int32
@@ -165,7 +168,12 @@
     ffn_expand,
     ffn_reduce,
 ):
-    count = inputs.shape[0] // lax.axis_size("feat")
+    inputs = gather_rows(inputs)
+    encoder = gather_rows(encoder)
+    output_grad = gather_rows(output_grad)
+    gains = lax.all_gather(gains, "feat", axis=1, tiled=True)
+    shifts = lax.all_gather(shifts, "feat", axis=1, tiled=True)
+    count = inputs.shape[0]
     width = self_outproj.shape[0]
     target_seg, target_valid = sentence_rows(target_lengths, count)
     source_seg, source_valid = sentence_rows(source_lengths, count)
@@ -262,7 +270,10 @@
     input_grad = grad_mid_one + part_one
     gain_local = jnp.stack([gain_one, gain_two, gain_three], axis=0)
     shift_local = jnp.stack([shift_one, shift_two, shift_three], axis=0)
-    gain_grad, shift_grad = lax.psum((gain_local, shift_local), "dp")
+    vectors = lax.psum(jnp.concatenate([gain_local, shift_local], axis=0), ("dp", "feat"))
+    half = vectors.shape[1] // lax.axis_size("feat")
+    vectors = lax.dynamic_slice_in_dim(vectors, lax.axis_index("feat") * half, half, axis=1)
+    gain_grad, shift_grad = vectors[:3], vectors[3:]
     weight_terms = (
         self_in_grad,
         self_out_grad,
@@ -272,51 +283,21 @@
         expand_grad,
         reduce_grad,
     )
-    summed_rows = (
-        lax.psum_scatter(weight_terms[0], "dp", scatter_dimension=0, tiled=True),
-        lax.psum_scatter(weight_terms[1], "dp", scatter_dimension=0, tiled=True),
-        lax.psum_scatter(weight_terms[2], "dp", scatter_dimension=0, tiled=True),
-        lax.psum_scatter(weight_terms[3], "dp", scatter_dimension=0, tiled=True),
-        lax.psum_scatter(weight_terms[4], "dp", scatter_dimension=0, tiled=True),
-        lax.psum_scatter(weight_terms[5], "dp", scatter_dimension=0, tiled=True),
-        lax.psum_scatter(weight_terms[6], "dp", scatter_dimension=0, tiled=True),
-    )
-    summed = (
-        lax.psum_scatter(
-            summed_rows[0].astype(jnp.bfloat16), "feat", scatter_dimension=1, tiled=True
-        ).astype(jnp.float32),
-        lax.psum_scatter(
-            summed_rows[1].astype(jnp.bfloat16), "feat", scatter_dimension=1, tiled=True
-        ).astype(jnp.float32),
-        lax.psum_scatter(
-            summed_rows[2].astype(jnp.bfloat16), "feat", scatter_dimension=1, tiled=True
-        ).astype(jnp.float32),
-        lax.psum_scatter(
-            summed_rows[3].astype(jnp.bfloat16), "feat", scatter_dimension=1, tiled=True
-        ).astype(jnp.float32),
-        lax.psum_scatter(
-            summed_rows[4].astype(jnp.bfloat16), "feat", scatter_dimension=1, tiled=True
-        ).astype(jnp.float32),
-        lax.psum_scatter(
-            summed_rows[5].astype(jnp.bfloat16), "feat", scatter_dimension=1, tiled=True
-        ).astype(jnp.float32),
-        lax.psum_scatter(
-            summed_rows[6].astype(jnp.bfloat16), "feat", scatter_dimension=1, tiled=True
-        ).astype(jnp.float32),
-    )
+    summed = []
+    for term in weight_terms:
+        pair = lax.psum_scatter(
+            term.astype(jnp.bfloat16), "feat", scatter_dimension=1, tiled=True
+        )
+        summed.append(
+            lax.psum_scatter(pair, "dp", scatter_dimension=0, tiled=True).astype(jnp.float32)
+        )
     return (
-        layer_out,
-        input_grad,
-        grad_source_cols.astype(jnp.float32),
+        spread_rows(layer_out),
+        spread_rows(input_grad),
+        spread_rows(grad_source_cols).astype(jnp.float32),
         gain_grad,
         shift_grad,
-        summed[0],
-        summed[1],
-        summed[2],
-        summed[3],
-        summed[4],
-        summed[5],
-        summed[6],
+        *summed,
     )
 
 

time: 1100 us -> 742 us (0.67)
  waiting for transfers between devices: 624 us -> 403 us
  blocking collectives: 106 us -> 44.6 us
  other arithmetic: 70.9 us -> 38.5 us
  starting transfers between devices: 46.8 us -> 27.4 us
  local copies, waits for them, and re-layouts: 69.7 us -> 58 us
    unnamed x24 -> x14, waiting for transfers between devices: 369 us -> 252 us
    reduce_scatter x4 -> x8, waiting for transfers between devices: 252 us -> 149 us  [the longest x1 130 us: per_device(): lax.psum_scatter(pair, 'dp', scatter_dimension=0, tiled=True)]
    psum x7 -> x1, blocking collectives: 97.2 us -> 40.8 us  [per_device(): lax.psum(jnp.concatenate([gain_local, shift_local], axis=0), ('dp', 'feat'))]
    all_to_all x12 -> x6, starting transfers between devices: 45.6 us -> 26.2 us  [the longest x3 13.3 us: spread_rows(): return lax.all_to_all(part, 'feat', split_axis=1, concat_axis=0, tiled=True)]
    convert_element_type x15 -> x5, other arithmetic: 22.3 us -> 5.71 us  [per_device(): lax.psum_scatter(pair, 'dp', scatter_dimension=0, tiled=True)]
    unnamed x131 -> x141, local copies, waits for them, and re-layouts: 40.7 us -> 30 us
  transfers between devices with their start and end apart: 26 -> 17, of which waited for: 14 -> 7; matrix products, arithmetic and copies ran while one was open for 17% -> 23% of each run, Pallas kernels for 0% -> 0%
where the time goes in v1:
time: 742 us; the launch traced here: 732 us
  waiting for transfers between devices  403 us (54%)
  matrix products  145 us (20%)
  local copies, waits for them, and re-layouts  58 us (8%)
  blocking collectives  44.6 us (6%)
  other arithmetic  38.5 us (5%)
  starting transfers between devices  27.4 us (4%)
  between operations  15.9 us (2%)
    unnamed x14, waiting for transfers between devices  252 us
    reduce_scatter x1, waiting for transfers between devices, per_device(): lax.psum_scatter(pair, 'dp', scatter_dimension=0, tiled=True)  130 us
    psum x1, blocking collectives, per_device(): lax.psum(jnp.concatenate([gain_local, shift_local], axis=0), ('dp', 'feat'))  40.8 us
    unnamed x141, local copies, waits for them, and re-layouts  30 us
    dot_general x7, matrix products, backward_product(): lax.dot_general(grad, weight, (((1,), (1,)), ((), ())), preferred_element...  28.6 us
    dot_general x7, matrix products, inner(): lax.dot_general(left, right, (((0,), (0,)), ((), ())), preferred_element_...  28.1 us
    dot_general x2, matrix products, attend_backward(): jnp.einsum('qhd,khd->hqk', grad_heads, split_heads(values), preferred_ele...  24.6 us
    reduce_scatter x7, waiting for transfers between devices, per_device(): lax.psum_scatter(term.astype(jnp.bfloat16), 'feat', scatter_dimension=1,...  19.4 us
  transfers between devices with their start and end apart: 17, of which 7 were waited for; matrix products, arithmetic and copies ran while one was open for 23% of the time, Pallas kernels for 0%

profile of v1, /device:TPU:0, one launch (start us, length us, event | category | flops | bytes accessed | tf_op | source)
XLA Modules:
  0.0 732.0 jit_solution(13034640641992369800)
XLA Ops:
  23.2 4.7 all-to-all-start
  38.0 4.7 all-to-all-start.3
  58.6 8.8 %fusion.79 = f32[640,3072]{1,0:T(8,128)} fusion(bf16[640,640]{0,1:T(8,128)(2,1)S(1)} %fusion.60, bf16[3072,640]{1,0:T(8,128)(2,1)} %param.27), kind=kOutput, calls=%fused_computation.178 | convolution fusion | flops 2516582400 | bytes 12615680 | tf_op jit(solution)/shard_map/dot_general | solution.py:30
  97.5 12.2 %fusion.7 = (bf16[640,3072]{1,0:T(8,128)(2,1)S(1)}, bf16[640,3072]{1,0:T(8,128)(2,1)}) fusion(f32[640,3072]{1,0:T(8,128)} %fusion.79, bf16[640,3072]{1,0:T(8,128)(2,1)S(1)} %copy-done.50, f32[640,640]{0,1:T(8,128)S(1)} %get-tuple-element.118, f32[640]{0:T(1024)S(1)} %get-tuple-element.91, f32[640]{0:T(1024)S(1)} %get-tuple-element.130, ...), kind=kOutput, calls=%fused_computation.24 | convolution fusion | flops 2561884160 | bytes 21309440 | tf_op jit(solution)/shard_map/dot_general | solution.py:221
  121.1 12.5 %multiply_reduce_fusion.1 = (f32[8,640]{1,0:T(8,128)S(1)}, f32[8,640,640]{1,2,0:T(8,128)}) fusion(f32[8,640,640]{1,2,0:T(8,128)} %copy-done.2, f32[8,640]{1,0:T(8,128)S(1)} %log_add_fusion.1, bf16[640,8,80]{0,2,1:T(8,128)(2,1)S(1)} %bitcast.172, bf16[640,8,80]{0,2,1:T(8,128)(2,1)} %bitcast.186), kind=kOutput, calls=%fused_computation.9 | convolution fusion | flops 534113280 | bytes 27893760 | tf_op jit(solution)/shard_map/qhd,khd->hqk/dot_general | solution.py:124
  133.6 6.6 multiply_convert_fusion.1
  153.0 5.6 multiply_convert_fusion.2
  158.6 7.3 fusion.52
  172.6 12.0 %multiply_reduce_fusion = (f32[8,640]{1,0:T(8,128)S(1)}, f32[8,640,640]{1,2,0:T(8,128)}) fusion(f32[8,640,640]{1,2,0:T(8,128)} %copy-done.1, f32[8,640]{1,0:T(8,128)S(1)} %log_add_fusion, bf16[640,8,80]{0,2,1:T(8,128)(2,1)S(1)} %bitcast.174, bf16[640,8,80]{0,2,1:T(8,128)(2,1)S(1)} %bitcast.184), kind=kOutput, calls=%fused_computation.6 | convolution fusion | flops 534113280 | bytes 27893760 | tf_op jit(solution)/shard_map/qhd,khd->hqk/dot_general | solution.py:124
  185.7 6.6 multiply_convert_fusion
  204.1 7.4 %convolution_convert_fusion = bf16[3072,640]{0,1:T(8,128)(2,1)} fusion(bf16[640,640]{0,1:T(8,128)(2,1)S(1)} %copy-done.34, bf16[640,3072]{1,0:T(8,128)(2,1)} %get-tuple-element.120), kind=kOutput, calls=%fused_computation.37 | convolution fusion | flops 2538209280 | bytes 8683520 | tf_op jit(solution)/shard_map/dot_general | solution.py:24
  211.6 8.3 %convolution_convert_fusion.1 = bf16[640,3072]{1,0:T(8,128)(2,1)} fusion(bf16[640,3072]{1,0:T(8,128)(2,1)} %copy-done.55, f32[640,640]{0,1:T(8,128)} %copy-done.18, f32[640]{0:T(1024)S(1)} %get-tuple-element.91, f32[640]{0:T(1024)S(1)} %get-tuple-element.130, f32[640]{0:T(1024)S(1)} %get-tuple-element.108, f32[640]{0:T(1024)S(1)} %get-tuple-element.107), kind=kOutput, calls=%fused_computation.38 | convolution fusion | flops 2520596480 | bytes 9512960 | tf_op jit(solution)/shard_map/dot_general | solution.py:24
  223.4 8.2 %reduce-scatter.33.cloned.1.call-done = bf16[3072,320]{0,1:T(8,128)(2,1)} async-done(((bf16[3072,640]{0,1:T(8,128)(2,1)}), bf16[3072,320]{0,1:T(8,128)(2,1)}) %reduce-scatter.33.cloned.1.call-update) | async-done | bytes 1966096 | tf_op jit(solution)/shard_map/reduce_scatter | solution.py:288
  231.6 4.1 copy.180
  235.8 11.1 %reduce-scatter.29.cloned.1.call-done = bf16[640,1536]{1,0:T(8,128)(2,1)} async-done(((bf16[640,3072]{1,0:T(8,128)(2,1)}), bf16[640,1536]{1,0:T(8,128)(2,1)}) %reduce-scatter.29.cloned.1.call-update) | async-done | bytes 1966096 | tf_op jit(solution)/shard_map/reduce_scatter | solution.py:288
  246.9 8.8 %convert_add_fusion.1 = f32[640,640]{0,1:T(8,128)} fusion(f32[640,640]{0,1:T(8,128)} %copy-done.18, bf16[3072,640]{1,0:T(8,128)(2,1)} %param.27, f32[640]{0:T(1024)S(1)} %fusion.61, bf16[640,3072]{1,0:T(8,128)(2,1)} %get-tuple-element.120), kind=kOutput, calls=%fused_computation.93 | convolution fusion | flops 2537881600 | bytes 11143680 | tf_op jit(solution)/shard_map/dot_general | solution.py:224
  255.8 4.8 all-to-all-start.2
  260.6 4.1 convolution_convert_fusion.7
  278.8 4.6 all-to-all-start.4
  290.2 40.8 %psum.7 = f32[6,640]{1,0:T(8,128)S(1)} all-reduce(f32[6,640]{1,0:T(8,128)S(1)} %concatenate.13), channel_id=1, replica_groups=mesh['dp'=16,'feat'=2] {'dp','feat'}, use_global_device_ids=true, to_apply=%region_28.29 | all-reduce | flops 3840 | bytes 30720 | tf_op jit(solution)/shard_map/psum | solution.py:273
  331.7 50.4 %all-reduce.7.cloned.1.call-done = (bf16[640,320]{0,1:T(8,128)(2,1)}, bf16[640,320]{0,1:T(8,128)(2,1)}, bf16[640,640]{0,1:T(8,128)(2,1)}, bf16[640,320]{0,1:T(8,128)(2,1)}) async-done(((bf16[640,320]{0,1:T(8,128)(2,1)}, bf16[640,320]{0,1:T(8,128)(2,1)}, bf16[640,640]{0,1:T(8,128)(2,1)}, bf16[640,320]{0,1:T(8,128)(2,1)}), (bf16[640,320]{0,1:T(8,128)(2,1)}, bf16[640,320]{0,1:T(8,128)(2,1)}, ...) | async-done | bytes 2048016
  389.2 73.2 %reduce-scatter.35.cloned.1.call-done = bf16[40,960]{1,0:T(8,128)(2,1)} async-done(((bf16[640,960]{1,0:T(8,128)(2,1)}), bf16[40,960]{1,0:T(8,128)(2,1)}) %reduce-scatter.35.cloned.1.call-update) | async-done | bytes 76816
  464.2 127.7 %reduce-scatter.37.cloned.1.call-done = bf16[192,320]{1,0:T(8,128)(2,1)} async-done(((bf16[3072,320]{1,0:T(8,128)(2,1)}), bf16[192,320]{1,0:T(8,128)(2,1)}) %reduce-scatter.37.cloned.1.call-update) | async-done | bytes 122896
  593.8 129.9 %reduce-scatter.31.cloned.1.call-done = bf16[40,1536]{1,0:T(8,128)(2,1)} async-done(((bf16[640,1536]{1,0:T(8,128)(2,1)}), bf16[40,1536]{1,0:T(8,128)(2,1)}) %reduce-scatter.31.cloned.1.call-update) | async-done | bytes 122896 | tf_op jit(solution)/shard_map/reduce_scatter | solution.py:292
  (261 shorter events, 151.7 us)
Async XLA Ops:
  7.2 40.5 %copy-start = (bf16[640,1920]{1,0:T(8,128)(2,1)S(1)}, bf16[640,1920]{1,0:T(8,128)(2,1)}, u32[]{:S(2)}) copy-start(bf16[640,1920]{1,0:T(8,128)(2,1)} %param.21) | copy-start | bytes 7372804
  9.5 13.7 %all-to-all-start.1 = ((bf16[2,640,320]{1,2,0:T(8,128)(2,1)}), bf16[2,640,320]{1,2,0:T(8,128)(2,1)S(1)}, u32[]{:S(2)}, u32[]{:S(2)}) async-start(bf16[2,640,320]{1,2,0:T(8,128)(2,1)} %bitcast.161), calls=%async_computation.1 | async-start | bytes 1638400 | tf_op jit(solution)/shard_map/all_to_all | solution.py:52
  23.2 14.9 %all-to-all-start = ((f32[2,640,320]{1,2,0:T(8,128)}), f32[2,640,320]{1,2,0:T(8,128)}, u32[]{:S(2)}, u32[]{:S(2)}) async-start(f32[2,640,320]{1,2,0:T(8,128)} %bitcast.177), calls=%async_computation | async-start | bytes 3276800 | tf_op jit(solution)/shard_map/all_to_all | solution.py:52
  38.0 19.0 %all-to-all-start.3 = ((f32[2,640,320]{1,2,0:T(8,128)}), f32[2,640,320]{1,2,0:T(8,128)}, u32[]{:S(2)}, u32[]{:S(2)}) async-start(f32[2,640,320]{1,2,0:T(8,128)} %bitcast.176), calls=%async_computation.3 | async-start | bytes 3276800 | tf_op jit(solution)/shard_map/all_to_all | solution.py:52
  42.7 177.3 %reduce-scatter.27.cloned.1.call-start = ((), (), s32[]{:S(2)}) async-start(), calls=%async_computation.20 | async-start | bytes 1228800 | tf_op jit(solution)/shard_map/reduce_scatter | solution.py:288
  96.4 16.9 %copy-start.18 = (f32[640,640]{0,1:T(8,128)}, f32[640,640]{0,1:T(8,128)S(1)}, u32[]{:S(2)}) copy-start(f32[640,640]{0,1:T(8,128)S(1)} %get-tuple-element.118) | copy-start | bytes 4915204
  118.4 101.7 %reduce-scatter.23.cloned.1.call-start = ((), (), s32[]{:S(2)}) async-start(), calls=%async_computation.18 | async-start | bytes 1228800 | tf_op jit(solution)/shard_map/reduce_scatter | solution.py:288
  121.0 12.6 %slice-start.4 = ((s8[13107200]{0:T(1024)(128)(4,1)}), s8[4194304]{0:T(1024)(128)(4,1)S(1)}, s32[]{:S(2)}) async-start(s8[13107200]{0:T(1024)(128)(4,1)} %bitcast.164), calls=%async_computation.31 | async-start | bytes 8388608
  121.0 12.6 %slice-start.5 = ((s8[13107200]{0:T(1024)(128)(4,1)}), s8[4194304]{0:T(1024)(128)(4,1)S(1)}, s32[]{:S(2)}) async-start(s8[13107200]{0:T(1024)(128)(4,1)} %bitcast.164), calls=%async_computation.32 | async-start | bytes 8388608
  121.0 12.5 %slice-start.6 = ((s8[13107200]{0:T(1024)(128)(4,1)}), s8[4194304]{0:T(1024)(128)(4,1)S(1)}, s32[]{:S(2)}) async-start(s8[13107200]{0:T(1024)(128)(4,1)} %bitcast.164), calls=%async_computation.33 | async-start | bytes 8388608
  145.9 74.2 %reduce-scatter.21.cloned.1.call-start = ((), (), s32[]{:S(2)}) async-start(), calls=%async_computation.17 | async-start | bytes 1228800 | tf_op jit(solution)/shard_map/reduce_scatter | solution.py:288
  153.0 67.1 %reduce-scatter.25.cloned.1.call-start = ((), (), s32[]{:S(2)}) async-start(), calls=%async_computation.19 | async-start | bytes 2457600 | tf_op jit(solution)/shard_map/reduce_scatter | solution.py:288
  169.6 51.2 %reduce-scatter.19.cloned.1.call-start = ((), (), s32[]{:S(2)}) async-start(), calls=%async_computation.16 | async-start | bytes 3686400 | tf_op jit(solution)/shard_map/reduce_scatter | solution.py:288
  172.5 13.1 %slice-start.2 = ((s8[13107200]{0:T(1024)(128)(4,1)}), s8[4194304]{0:T(1024)(128)(4,1)S(1)}, s32[]{:S(2)}) async-start(s8[13107200]{0:T(1024)(128)(4,1)} %bitcast.162), calls=%async_computation.29 | async-start | bytes 8388608
  172.6 13.2 %slice-start.3 = ((s8[13107200]{0:T(1024)(128)(4,1)}), s8[524288]{0:T(1024)(128)(4,1)S(1)}, s32[]{:S(2)}) async-start(s8[13107200]{0:T(1024)(128)(4,1)} %bitcast.162), calls=%async_computation.30 | async-start | bytes 1048576
  203.0 28.6 %reduce-scatter.33.cloned.1.call-start = ((), (), s32[]{:S(2)}) async-start(), calls=%async_computation.23 | async-start | bytes 5898240 | tf_op jit(solution)/shard_map/reduce_scatter | solution.py:288
  211.5 35.4 %reduce-scatter.29.cloned.1.call-start = ((), (), s32[]{:S(2)}) async-start(), calls=%async_computation.21 | async-start | bytes 5898240 | tf_op jit(solution)/shard_map/reduce_scatter | solution.py:288
  220.0 162.1 %all-reduce.7.cloned.1.call-start = ((), (), s32[]{:S(2)}) async-start(), calls=%async_computation.26 | async-start | bytes 4096000
  220.7 241.6 %reduce-scatter.35.cloned.1.call-start = ((), (), s32[]{:S(2)}) async-start(), calls=%async_computation.24 | async-start | bytes 1392640
  223.4 368.6 %reduce-scatter.37.cloned.1.call-start = ((), (), s32[]{:S(2)}) async-start(), calls=%async_computation.25 | async-start | bytes 2506752
  235.8 487.9 %reduce-scatter.31.cloned.1.call-start = ((), (), s32[]{:S(2)}) async-start(), calls=%async_computation.22 | async-start | bytes 2088960 | tf_op jit(solution)/shard_map/reduce_scatter | solution.py:292
  255.8 8.9 %all-to-all-start.2 = ((f32[640,2,320]{0,2,1:T(8,128)}), f32[640,2,320]{0,2,1:T(8,128)}, u32[]{:S(2)}, u32[]{:S(2)}) async-start(f32[640,2,320]{0,2,1:T(8,128)} %bitcast.198), calls=%async_computation.2 | async-start | bytes 3276800 | tf_op jit(solution)/shard_map/all_to_all | solution.py:56
  264.7 14.2 %all-to-all-start.5 = ((bf16[640,2,320]{0,2,1:T(8,128)(2,1)}), bf16[640,2,320]{0,2,1:T(8,128)(2,1)S(1)}, u32[]{:S(2)}, u32[]{:S(2)}) async-start(bf16[640,2,320]{0,2,1:T(8,128)(2,1)} %bitcast.202), calls=%async_computation.5 | async-start | bytes 1638400 | tf_op jit(solution)/shard_map/all_to_all | solution.py:56
  278.8 7.3 all-to-all-start.4
  (57 other events, 269.9 us)
Sparse Core Ops, SparseCore 0:
  118.5 11.1 reduce-scatter.26
  146.0 11.1 reduce-scatter.22
  159.5 9.4 reduce-scatter.20
  171.7 10.2 reduce-scatter.24
  203.1 13.1 reduce-scatter.18
  218.5 13.0 reduce-scatter.32
  233.8 13.0 reduce-scatter.28
  253.9 128.1 all-reduce.6
  384.3 77.9 reduce-scatter.34
  467.1 124.7 reduce-scatter.36
  597.5 126.0 reduce-scatter.30
